TPU v7x, 32 devices: a whole 2x2x4 slice. The times are simulated.
32 devices in a mesh: dp: 8 (over z, x), date: 4 (over y, core).
Axes of the slice: x: 2, y: 2, z: 4, core: 2. Of those that a mesh axis runs over, the one named last changes fastest.
Arguments:
- inputs: bfloat16 [8, 16, 32, 512], P('dp', 'date'), may hold values from -6 to 6
- pre_act: bfloat16 [8, 16, 32, 2048], P('dp', 'date'), may hold values from -6 to 6
- hidden_grad: bfloat16 [8, 16, 32, 2048], P('dp', 'date'), may hold values from -6 to 6
- weight_in: bfloat16 [512, 2048], replicated, may hold values from -0.125 to 0.125
- error_in: bfloat16 [8, 512, 2048], P('dp', 'date'), may hold values from -2 to 2, as said below
- q_prev: float32 [2048, 64], replicated, may hold values from -6 to 6
Outputs:
- input_grad: bfloat16 [8, 16, 32, 512], P('dp', None, 'date')
- p_hat: float32 [512, 64], P('date')
- q_new: float32 [2048, 64], replicated
- error_out: bfloat16 [8, 512, 2048], P('dp', 'date')
Inputs may be any that keep to these rules, and one draw needn't show every extreme that they name: `error_in`: each group's buffer is a part common to all groups plus a part of its own.
All inputs are finite; a program needn't handle non-finite values.
Results may differ from a plain program's by a relative error of at most 0.005.
Values may be sent and summed in bfloat16 or wider, within the bound.
A program may use at most 64 MiB of HBM per device.

v0:
```python
import jax
import jax.numpy as jnp
from jax import lax
from jax.sharding import PartitionSpec as P

inv_root2 = 0.7071067811865476
inv_root_twopi = 0.3989422804014327
highest = lax.Precision.HIGHEST


def gelu_slope(pre_act):
    value = pre_act.astype(jnp.float32)
    return (
        0.5 * (1.0 + lax.erf(value * inv_root2))
        + value * jnp.exp(-0.5 * value * value) * inv_root_twopi
    )


def orthonormal(proj, gram_matrix):
    factor = jnp.linalg.cholesky(gram_matrix)
    return jax.scipy.linalg.solve_triangular(factor, proj.T, lower=True).T


def local(inputs, pre_act, hidden_grad, weight_in, error_in, q_prev):
    date_count = lax.axis_size("date")
    width_in = inputs.shape[-1]
    width_hidden = pre_act.shape[-1]
    token_rows = inputs.reshape(-1, width_in)
    grad_scale = (token_rows.shape[0] * date_count) ** (-0.5)
    slope_grad = (
        hidden_grad.reshape(-1, width_hidden).astype(jnp.float32)
        * gelu_slope(pre_act.reshape(-1, width_hidden))
    ).astype(jnp.bfloat16)
    local_back = lax.dot_general(
        slope_grad, weight_in, (((1,), (1,)), ((), ())), preferred_element_type=jnp.float32
    ).astype(jnp.bfloat16)
    input_grad = lax.all_to_all(
        local_back.reshape(inputs.shape), "date", split_axis=2, concat_axis=1, tiled=True
    )
    column_block = lax.all_to_all(token_rows, "date", split_axis=1, concat_axis=0, tiled=True)
    own_grad = grad_scale * lax.dot_general(
        column_block,
        lax.all_gather(slope_grad, "date", axis=0, tiled=True),
        (((0,), (0,)), ((), ())),
        preferred_element_type=jnp.float32,
    )
    own_error = error_in[0].astype(jnp.float32)
    merged_rows = own_error + own_grad
    proj_rows = lax.psum(jnp.dot(merged_rows, q_prev, precision=highest), "dp")
    gram_matrix = lax.psum(jnp.dot(proj_rows.T, proj_rows, precision=highest), "date")
    p_rows = orthonormal(proj_rows, gram_matrix)
    right_part = jnp.dot(merged_rows.T, p_rows, precision=highest)
    q_new = lax.psum(right_part, ("dp", "date")) / lax.axis_size("dp")
    error_out = (merged_rows - jnp.dot(p_rows, q_new.T, precision=highest)).astype(jnp.bfloat16)[
        None
    ]
    return (input_grad, p_rows, q_new, error_out)


def solution(mesh):
    in_specs = (
        P("dp", "date", None, None),
        P("dp", "date", None, None),
        P("dp", "date", None, None),
        P(),
        P("dp", "date", None),
        P(),
    )
    out_specs = (P("dp", None, "date", None), P("date", None), P(), P("dp", "date", None))
    return jax.shard_map(local, mesh=mesh, in_specs=in_specs, out_specs=out_specs, check_vma=False)
```

profile of v0, /device:TPU:1, one launch (start us, length us, event | category | flops | bytes accessed | tf_op | source)
XLA Modules:
  0.0 237.2 jit_solution(10452233172017301565)
XLA Ops:
  7.2 0.0 copy-start
  7.2 0.0 all-gather.2.cloned.1.call-start
  7.2 2.6 %fusion.11 = bf16[128,2048]{1,0:T(8,128)(2,1)} fusion(bf16[1,4,32,2048]{3,2,1,0:T(8,128)(2,1)} %param.8, bf16[1,4,32,2048]{3,2,1,0:T(8,128)(2,1)} %param.7), kind=kLoop, calls=%fused_computation.18 | loop fusion | flops 3145728 | bytes 1572864 | tf_op jit(solution)/shard_map/convert_element_type | solution.py:33
  9.9 0.0 all-gather.2.cloned.1.call-update
  10.0 0.7 copy.32
  10.6 4.3 %all-to-all-start.1 = ((bf16[128,4,128]{2,0,1:T(8,128)(2,1)}), bf16[128,4,128]{2,0,1:T(8,128)(2,1)S(1)}, u32[]{:S(2)}, u32[]{:S(2)}) async-start(bf16[128,4,128]{2,0,1:T(8,128)(2,1)} %copy.32), calls=%async_computation.1 | async-start | bytes 262144 | tf_op jit(solution)/shard_map/all_to_all | solution.py:40
  14.9 1.0 copy.31
  15.9 2.6 %all-to-all-done.1 = bf16[128,4,128]{2,0,1:T(8,128)(2,1)S(1)} async-done(((bf16[128,4,128]{2,0,1:T(8,128)(2,1)}), bf16[128,4,128]{2,0,1:T(8,128)(2,1)S(1)}, u32[]{:S(2)}, u32[]{:S(2)}) %all-to-all-start.1) | async-done | bytes 131104 | tf_op jit(solution)/shard_map/all_to_all | solution.py:40
  18.5 16.8 %all-gather.2.cloned.1.call-done = bf16[512,2048]{1,0:T(8,128)(2,1)} async-done(((bf16[128,2048]{1,0:T(8,128)(2,1)}), bf16[512,2048]{1,0:T(8,128)(2,1)}) %all-gather.2.cloned.1.call-update) | async-done | bytes 2097168 | tf_op jit(solution)/shard_map/all_gather | solution.py:43
  35.3 2.5 %fusion.1 = f32[128,2048]{0,1:T(8,128)S(1)} fusion(bf16[512,2048]{1,0:T(8,128)(2,1)} %all-gather.2.cloned.1.call-done, bf16[512,128]{1,0:T(8,128)(2,1)S(1)} %bitcast.48, bf16[1,128,2048]{1,2,0:T(8,128)(2,1)} %copy.31), kind=kOutput, calls=%fused_computation.3 | convolution fusion | flops 269221888 | bytes 3801088 | tf_op jit(solution)/shard_map/dot_general | solution.py:41
  37.8 0.8 fusion.16
  38.5 29.9 %psum.21 = f32[128,64]{0,1:T(8,128)S(1)} all-reduce(f32[128,64]{0,1:T(8,128)S(1)} %fusion.16), channel_id=1, replica_groups=mesh['dp'=8,'date'=4] {'dp'}, use_global_device_ids=true, to_apply=%region_0.0 | all-reduce | flops 8192 | bytes 65536 | tf_op jit(solution)/shard_map/psum | solution.py:49
  68.4 0.2 fusion.17
  68.6 17.0 %psum.22 = f32[64,64]{0,1:T(8,128)S(1)} all-reduce(f32[64,64]{0,1:T(8,128)S(1)} %fusion.17), channel_id=1, replica_groups=mesh['dp'=8,'date'=4] {'date'}, use_global_device_ids=true, to_apply=%region_1.0 | all-reduce | flops 4096 | bytes 32768 | tf_op jit(solution)/shard_map/psum | solution.py:50
  85.6 0.1 copy.34
  85.7 5.8 %cholesky.16 = f32[64,64]{1,0:T(8,128)S(1)} custom-call(f32[64,64]{1,0:T(8,128)S(1)} %fusion.15), custom_call_target="Cholesky" | custom-call | tf_op jit(solution)/shard_map/jit(cholesky)/cholesky | solution.py:20
  91.6 0.6 compare_reduce_fusion
  92.2 0.7 fusion.12
  92.9 4.9 %custom-call.7 = f32[1,64,64]{1,2,0:T(8,128)S(1)} custom-call(f32[1,64,64]{2,1,0:T(8,128)S(1)} %fusion.12), custom_call_target="InvertDiagBlocksLowerTriangular" | custom-call | tf_op jit(solution)/shard_map/jit(_solve_triangular)/triangular_solve | solution.py:21
  97.8 0.3 fusion.13
  98.1 0.0 copy-start.4
  98.1 2.1 fusion.18
  100.1 0.0 all-reduce.2.cloned.1.call-update
  100.2 1.9 convolution_convert_fusion
  102.0 0.1 copy.29
  102.2 7.5 %all_to_all.37 = bf16[1,4,32,512]{3,1,0,2:T(4,128)(2,1)S(1)} all-to-all(bf16[1,4,32,512]{3,1,0,2:T(4,128)(2,1)S(1)} %copy.29), channel_id=1, replica_groups=mesh['dp'=8,'date'=4] {'date'}, dimensions={2} | all-to-all | bytes 262144 | tf_op jit(solution)/shard_map/all_to_all | solution.py:37
  109.6 0.7 copy.30
  110.3 113.5 %all-reduce.2.cloned.1.call-done = f32[2048,64]{0,1:T(8,128)} async-done(((f32[2048,64]{0,1:T(8,128)}), f32[2048,64]{0,1:T(8,128)}) %all-reduce.2.cloned.1.call-update) | async-done | bytes 524304 | tf_op jit(solution)/shard_map/psum | solution.py:53
  223.8 1.1 broadcast_multiply_fusion
  224.9 0.8 copy-done.1
  225.7 2.6 %fusion.3 = bf16[1,128,2048]{1,2,0:T(8,128)(2,1)} fusion(f32[128,2048]{0,1:T(8,128)S(1)} %fusion.1, f32[64,128]{1,0:T(8,128)S(1)} %fusion.13, f32[2048,64]{0,1:T(8,128)S(1)} %broadcast_multiply_fusion), kind=kOutput, calls=%fused_computation.5 | convolution fusion | flops 201850880 | bytes 2129920 | tf_op jit(solution)/shard_map/dot_general | solution.py:54
  228.3 2.0 copy.36
  (13 shorter events, 0.1 us)
Async XLA Ops:
  7.2 93.0 %copy-start = (bf16[512,2048]{1,0:T(8,128)(2,1)S(1)}, bf16[512,2048]{1,0:T(8,128)(2,1)}, u32[]{:S(2)}) copy-start(bf16[512,2048]{1,0:T(8,128)(2,1)} %param.9) | copy-start | bytes 6291460
  7.2 2.7 %copy-start.5 = (bf16[1,4,32,512]{3,2,1,0:T(8,128)(2,1)S(1)}, bf16[1,4,32,512]{3,2,1,0:T(8,128)(2,1)}, u32[]{:S(2)}) copy-start(bf16[1,4,32,512]{3,2,1,0:T(8,128)(2,1)} %param.6) | copy-start | bytes 393220
  7.2 7.7 %copy-start.3 = (bf16[1,128,2048]{2,1,0:T(8,128)(2,1)S(1)}, bf16[1,128,2048]{2,1,0:T(8,128)(2,1)}, u32[]{:S(2)}) copy-start(bf16[1,128,2048]{2,1,0:T(8,128)(2,1)} %param.10) | copy-start | bytes 1572868
  7.2 28.1 %all-gather.2.cloned.1.call-start = ((), (), s32[]{:S(2)}) async-start(), calls=%async_computation.2 | async-start | bytes 2621440 | tf_op jit(solution)/shard_map/all_gather | solution.py:43
  10.6 7.9 %all-to-all-start.1 = ((bf16[128,4,128]{2,0,1:T(8,128)(2,1)}), bf16[128,4,128]{2,0,1:T(8,128)(2,1)S(1)}, u32[]{:S(2)}, u32[]{:S(2)}) async-start(bf16[128,4,128]{2,0,1:T(8,128)(2,1)} %copy.32), calls=%async_computation.1 | async-start | bytes 262144 | tf_op jit(solution)/shard_map/all_to_all | solution.py:40
  14.9 208.9 %all-reduce.2.cloned.1.call-start = ((), (), s32[]{:S(2)}) async-start(), calls=%async_computation.3 | async-start | bytes 1048576 | tf_op jit(solution)/shard_map/psum | solution.py:53
  35.3 2.5 %copy-start.2 = (f32[2048,64]{0,1:T(8,128)S(1)}, f32[2048,64]{0,1:T(8,128)}, u32[]{:S(2)}) copy-start(f32[2048,64]{0,1:T(8,128)} %param.11) | copy-start | bytes 1572868
  98.1 126.8 %copy-start.4 = (f32[64,128]{1,0:T(8,128)}, f32[64,128]{1,0:T(8,128)S(1)}, u32[]{:S(2)}) copy-start(f32[64,128]{1,0:T(8,128)S(1)} %fusion.13) | copy-start | bytes 98308
  224.9 0.8 copy-start.1
Sparse Core Ops, SparseCore 0:
  10.2 25.0 all-gather.1
  100.3 123.4 all-reduce.1
where the time goes:
time: 239 us; the launch traced here: 237 us
  waiting for transfers between devices  133 us (56%)
  blocking collectives  54.3 us (23%)
  other arithmetic  15.8 us (7%)
  between operations  14.2 us (6%)
  matrix products  10.2 us (4%)
  local copies, waits for them, and re-layouts  5.43 us (2%)
  starting transfers between devices  4.33 us (2%)
    psum x1, waiting for transfers between devices, local(): q_new = lax.psum(right_part, ('dp', 'date')) / lax.axis_size('dp')  114 us
    psum x1, blocking collectives, local(): proj_rows = lax.psum(jnp.dot(merged_rows, q_prev, precision=highest), 'dp')  29.9 us
    psum x1, blocking collectives, local(): lax.psum(jnp.dot(proj_rows.T, proj_rows, precision=highest), 'date')  17 us
    all_gather x1, waiting for transfers between devices, local(): lax.all_gather(slope_grad, 'date', axis=0, tiled=True)  16.8 us
    all_to_all x1, blocking collectives, local(): lax.all_to_all(local_back.reshape(inputs.shape), 'date', split_axis=2, co...  7.46 us
    another operation x3, other arithmetic, orthonormal(): factor = jnp.linalg.cholesky(gram_matrix)  6.52 us
    another operation x2, other arithmetic, orthonormal(): return jax.scipy.linalg.solve_triangular(factor, proj.T, lower=True).T  5.55 us
  transfers between devices with their start and end apart: 3, of which 3 were waited for; matrix products, arithmetic and copies ran while one was open for 2% of the time, Pallas kernels for 0%

commit v1 on v0

--- a/solution.py
+++ b/solution.py
@@ -1,11 +1,18 @@
+import functools
+
 import jax
 import jax.numpy as jnp
 from jax import lax
+from jax.experimental import pallas as pl
+from jax.experimental.pallas import tpu as pltpu
 from jax.sharding import PartitionSpec as P
 
 inv_root2 = 0.7071067811865476
 inv_root_twopi = 0.3989422804014327
 highest = lax.Precision.HIGHEST
+MESH = pl.DeviceIdType.MESH
+f32 = jnp.float32
+bf16 = jnp.bfloat16
 
 
 def gelu_slope(pre_act):
@@ -16,12 +23,386 @@
     )
 
 
+def dot(a, b, ca, cb, precision=None):
+    return lax.dot_general(
+        a, b, (((ca,), (cb,)), ((), ())), preferred_element_type=f32, precision=precision
+    )
+
+
+def parts(value):
+    high = value.astype(bf16)
+    return high, (value - high.astype(f32)).astype(bf16)
+
+
+def whiten(proj_t):
+    rank = proj_t.shape[0]
+    gram = dot(proj_t, proj_t, 1, 1, highest)
+    rows = lax.broadcasted_iota(jnp.int32, (rank, rank), 0)
+    cols = lax.broadcasted_iota(jnp.int32, (rank, rank), 1)
+    eye = (rows == cols).astype(f32)
+    table = jnp.concatenate([gram, eye], axis=1)
+    blocks = [table[8 * i : 8 * i + 8] for i in range(rank // 8)]
+    sub = lax.broadcasted_iota(jnp.int32, (8, 2 * rank), 0)
+    for k in range(rank):
+        i, r = divmod(k, 8)
+        row = blocks[i][r : r + 1, :]
+        row = row * (1.0 / row[:, k : k + 1])
+        for j in range(i, rank // 8):
+            update = blocks[j][:, k : k + 1] * row
+            if j == i:
+                update = jnp.where(sub > r, update, 0.0)
+            blocks[j] = blocks[j] - update
+    table = jnp.concatenate(blocks, axis=0)
+    pivots = jnp.sum(table[:, :rank] * eye, axis=1, keepdims=True)
+    return dot(table[:, rank:] * lax.rsqrt(pivots), proj_t, 1, 0, highest)
+
+
+def kernel(
+    n_dp,
+    n_date,
+    patches,
+    x_hbm,
+    pre_hbm,
+    hid_hbm,
+    w_hbm,
+    err_hbm,
+    q_hbm,
+    ig_ref,
+    p_ref,
+    qn_ref,
+    eo_ref,
+    x_v,
+    pre_v,
+    hid_v,
+    w_v,
+    stack,
+    q_v,
+    slopes,
+    xcols,
+    back_send,
+    back_recv,
+    proj_part,
+    proj_recv,
+    proj_full,
+    p_full,
+    right_send,
+    right_recv,
+    right_full,
+    merged,
+    load_sem,
+    slope_send,
+    slope_recv,
+    xcol_send,
+    xcol_recv,
+    ig_send,
+    ig_recv,
+    pr_send,
+    pr_recv,
+    pg_send,
+    pg_recv,
+    qr_send,
+    qr_recv,
+    qg_send,
+    qg_recv,
+):
+    tokens, width_in = x_v.shape
+    width_hidden = stack.shape[1]
+    rank = q_v.shape[1]
+    cols_own = width_in // n_date
+    scale = (tokens * n_date) ** (-0.5)
+    pa = rank // n_dp
+    qa, qb = width_hidden // n_dp, rank // n_date
+    half = tokens // 2
+    dp = lax.axis_index("dp")
+    date = lax.axis_index("date")
+    others = [(i, j) for i in range(n_dp) for j in range(n_date) if i + j > 0]
+    others = sorted(others, key=lambda o: -min(o[0], n_dp - o[0]))
+
+    def slot(o):
+        return o[0] * n_date + o[1]
+
+    def target(o):
+        return lax.rem(dp + o[0], n_dp), lax.rem(date + o[1], n_date)
+
+    loads = []
+    for c in range(2):
+        for h, v in ((pre_hbm, pre_v), (hid_hbm, hid_v)):
+            rows = pl.ds(c * half, half)
+            loads.append((h.at[rows], v.at[rows]))
+    loads.append((q_hbm, q_v))
+    loads.append((err_hbm, stack.at[pl.ds(tokens, cols_own)]))
+    loads.append((x_hbm, x_v))
+    loads.append((w_hbm, w_v))
+    loads = [pltpu.make_async_copy(s, d, load_sem.at[n]) for n, (s, d) in enumerate(loads)]
+    for copy in loads:
+        copy.start()
+
+    barrier = pltpu.get_barrier_semaphore()
+    for o in others:
+        pl.semaphore_signal(barrier, inc=1, device_id=target(o), device_id_type=MESH)
+
+    def remote(src, dst, send, recv, device):
+        return pltpu.make_async_remote_copy(
+            src_ref=src,
+            dst_ref=dst,
+            send_sem=send,
+            recv_sem=recv,
+            device_id=device,
+            device_id_type=MESH,
+        )
+
+    mate = date + 1 - 2 * lax.rem(date, 2)
+    across = lax.rem(date + 2, n_date)
+    diag = lax.rem(mate + 2, n_date)
+    sent = []
+
+    def slope_copy(c, kind):
+        rows = pl.ds(c * half, half)
+        src = stack.at[rows] if kind < 2 else slopes.at[1, rows]
+        device = (dp, across if kind == 1 else mate)
+        n = 2 * kind + c
+        return remote(src, slopes.at[kind, rows], slope_send.at[n], slope_recv.at[n], device)
+
+    for c in range(2):
+        loads[2 * c].wait()
+        loads[2 * c + 1].wait()
+        for s in range(half // 16):
+            rows = pl.ds(c * half + s * 16, 16)
+            stack[rows, :] = (hid_v[rows, :].astype(f32) * gelu_slope(pre_v[rows, :])).astype(bf16)
+        if c == 0:
+            pl.semaphore_wait(barrier, len(others))
+        for kind in (1, 0):
+            copy = slope_copy(c, kind)
+            copy.start()
+            sent.append(copy)
+
+    loads[4].wait()
+    loads[5].wait()
+    q_high, q_low = parts(q_v[...])
+    both = stack[...]
+    seen = dot(both, q_high, 1, 0) + dot(both, q_low, 1, 0)
+    loads[6].wait()
+    x = x_v[...]
+    y_high, y_low = parts(seen[:tokens] * scale)
+    proj_part[...] = dot(y_high, x, 0, 0) + dot(y_low, x, 0, 0)
+    own_cols = pl.ds(pl.multiple_of(date * cols_own, cols_own), cols_own)
+    proj_part[:, own_cols] += seen[tokens:].T
+
+    def proj_tile(ref, i, j):
+        return ref.at[
+            pl.ds(pl.multiple_of(i * pa, pa), pa),
+            pl.ds(pl.multiple_of(j * cols_own, cols_own), cols_own),
+        ]
+
+    reduce_copies = []
+    for o in others:
+        n = slot(o)
+        to = target(o)
+        copy = remote(
+            proj_tile(proj_part, *to), proj_recv.at[n], pr_send.at[n], pr_recv.at[n], to
+        )
+        copy.start()
+        reduce_copies.append(copy)
+        sent.append(copy)
+
+    x_copies, ig_copies = [], []
+    for off in range(1, n_date):
+        peer = lax.rem(date + off, n_date)
+        cols = pl.ds(pl.multiple_of(peer * cols_own, cols_own), cols_own)
+        copy = remote(
+            x_v.at[:, cols], xcols.at[off], xcol_send.at[off], xcol_recv.at[off], (dp, peer)
+        )
+        copy.start()
+        x_copies.append(copy)
+        sent.append(copy)
+    loads[7].wait()
+    back = dot(stack[:tokens, :], w_v[...], 1, 1)
+    dates = tokens // (patches * n_date)
+    for j in range(n_date):
+        pieces = [
+            back[d * n_date * patches + j * patches : d * n_date * patches + (j + 1) * patches]
+            for d in range(dates)
+        ]
+        back_send[j] = jnp.concatenate(pieces, axis=0).astype(bf16)
+    for off in range(1, n_date):
+        peer = lax.rem(date + off, n_date)
+        copy = remote(
+            back_send.at[peer], back_recv.at[off], ig_send.at[off], ig_recv.at[off], (dp, peer)
+        )
+        copy.start()
+        ig_copies.append(copy)
+        sent.append(copy)
+
+    total = proj_tile(proj_part, dp, date)[...]
+    for o, copy in zip(others, reduce_copies):
+        copy.wait_recv()
+        total = total + proj_recv[slot(o)]
+    mine = proj_tile(proj_full, dp, date)
+    mine[...] = total
+    for o in others:
+        n = slot(o)
+        copy = remote(mine, mine, pg_send.at[n], pg_recv.at[n], target(o))
+        copy.start()
+        sent.append(copy)
+
+    xcol = x_v[:, own_cols]
+    merged[...] = stack[tokens:, :].astype(f32) + dot(xcol, stack[:tokens, :], 0, 0) * scale
+
+    for o in others:
+        n = slot(o)
+        source = (lax.rem(dp - o[0] + n_dp, n_dp), lax.rem(date - o[1] + n_date, n_date))
+        tile = proj_tile(proj_full, *source)
+        remote(tile, tile, pg_send.at[n], pg_recv.at[n], target(o)).wait_recv()
+    p_all = whiten(proj_full[...])
+    p_full[...] = p_all
+    p_own = p_full[:, own_cols]
+    p_ref[...] = p_own
+    p_high, p_low = parts(p_all)
+    z = (dot(p_high, x, 1, 1) + dot(p_low, x, 1, 1)) * scale
+    left_high, left_low = parts(jnp.concatenate([z, p_own], axis=1))
+    right = dot(left_high, both, 1, 0) + dot(left_low, both, 1, 0)
+    right_send[...] = right.astype(bf16)
+
+    def right_tile(ref, i, j):
+        return ref.at[
+            pl.ds(pl.multiple_of(j * qb, qb), qb), pl.ds(pl.multiple_of(i * qa, qa), qa)
+        ]
+
+    reduce_copies = []
+    for o in others:
+        n = slot(o)
+        to = target(o)
+        copy = remote(
+            right_tile(right_send, *to), right_recv.at[n], qr_send.at[n], qr_recv.at[n], to
+        )
+        copy.start()
+        reduce_copies.append(copy)
+        sent.append(copy)
+
+    for c in range(2):
+        slope_copy(c, 1).wait_recv()
+        copy = slope_copy(c, 2)
+        copy.start()
+        sent.append(copy)
+    for copy in x_copies:
+        copy.wait_recv()
+
+    def add_peer(kind, peer):
+        off = lax.rem(date - peer + n_date, n_date)
+        return dot(xcols[off], slopes[kind], 0, 0) * scale
+
+    for c in range(2):
+        slope_copy(c, 0).wait_recv()
+    merged[...] += add_peer(0, mate) + add_peer(1, across)
+
+    total = right_tile(right_send, dp, date)[...].astype(f32)
+    for o, copy in zip(others, reduce_copies):
+        copy.wait_recv()
+        total = total + right_recv[slot(o)].astype(f32)
+    mine = right_tile(right_full, dp, date)
+    mine[...] = (total * (1.0 / n_dp)).astype(bf16)
+    for o in others:
+        n = slot(o)
+        copy = remote(mine, mine, qg_send.at[n], qg_recv.at[n], target(o))
+        copy.start()
+        sent.append(copy)
+
+    ig_rows = back_send.shape[1]
+    for off, copy in zip(range(1, n_date), ig_copies):
+        copy.wait_recv()
+        source = lax.rem(date - off + n_date, n_date)
+        ig_ref[pl.ds(pl.multiple_of(source * ig_rows, ig_rows), ig_rows), :] = back_recv[off]
+    ig_ref[pl.ds(pl.multiple_of(date * ig_rows, ig_rows), ig_rows), :] = back_send[date]
+    for c in range(2):
+        slope_copy(c, 2).wait_recv()
+    merged[...] += add_peer(2, diag)
+    own_high, own_low = parts(p_own)
+
+    for o in others:
+        n = slot(o)
+        source = (lax.rem(dp - o[0] + n_dp, n_dp), lax.rem(date - o[1] + n_date, n_date))
+        tile = right_tile(right_full, *source)
+        remote(tile, tile, qg_send.at[n], qg_recv.at[n], target(o)).wait_recv()
+    q_new = right_full[...]
+    qn_ref[...] = q_new
+    low_rank = dot(own_high, q_new, 0, 0) + dot(own_low, q_new, 0, 0)
+    eo_ref[...] = (merged[...] - low_rank).astype(bf16)
+    for copy in sent:
+        copy.wait_send()
+
+
+def fused(n_dp, n_date, inputs, pre_act, hidden_grad, weight_in, error_in, q_prev):
+    width_in, width_hidden = weight_in.shape
+    rank = q_prev.shape[1]
+    x = inputs.reshape(-1, width_in)
+    tokens = x.shape[0]
+    n = n_dp * n_date
+    cols_own = width_in // n_date
+    patches = inputs.shape[2] // n_date
+    ig_rows = inputs.shape[1] * patches
+    any_spec = pl.BlockSpec(memory_space=pl.ANY)
+    vmem_spec = pl.BlockSpec(memory_space=pltpu.VMEM)
+    dma = pltpu.SemaphoreType.DMA
+    qa, qb = width_hidden // n_dp, rank // n_date
+    ig, p_t, q_t, eo = pl.pallas_call(
+        functools.partial(kernel, n_dp, n_date, patches),
+        out_shape=(
+            jax.ShapeDtypeStruct((n_date * ig_rows, width_in), bf16),
+            jax.ShapeDtypeStruct((rank, cols_own), f32),
+            jax.ShapeDtypeStruct((rank, width_hidden), bf16),
+            jax.ShapeDtypeStruct((cols_own, width_hidden), bf16),
+        ),
+        in_specs=[any_spec] * 6,
+        out_specs=(vmem_spec,) * 4,
+        scratch_shapes=[
+            pltpu.VMEM((tokens, width_in), bf16),
+            pltpu.VMEM((tokens, width_hidden), bf16),
+            pltpu.VMEM((tokens, width_hidden), bf16),
+            pltpu.VMEM((width_in, width_hidden), bf16),
+            pltpu.VMEM((tokens + cols_own, width_hidden), bf16),
+            pltpu.VMEM((width_hidden, rank), f32),
+            pltpu.VMEM((3, tokens, width_hidden), bf16),
+            pltpu.VMEM((n_date, tokens, cols_own), bf16),
+            pltpu.VMEM((n_date, ig_rows, width_in), bf16),
+            pltpu.VMEM((n_date, ig_rows, width_in), bf16),
+            pltpu.VMEM((rank, width_in), f32),
+            pltpu.VMEM((n, rank // n_dp, cols_own), f32),
+            pltpu.VMEM((rank, width_in), f32),
+            pltpu.VMEM((rank, width_in), f32),
+            pltpu.VMEM((rank, width_hidden), bf16),
+            pltpu.VMEM((n, qb, qa), bf16),
+            pltpu.VMEM((rank, width_hidden), bf16),
+            pltpu.VMEM((cols_own, width_hidden), f32),
+            dma((8,)),
+            dma((6,)),
+            dma((6,)),
+            dma((n_date,)),
+            dma((n_date,)),
+            dma((n_date,)),
+            dma((n_date,)),
+        ]
+        + [dma((n,))] * 8,
+        compiler_params=pltpu.CompilerParams(
+            collective_id=0, has_side_effects=True, vmem_limit_bytes=48 * 1024 * 1024
+        ),
+    )(
+        x,
+        pre_act.reshape(tokens, width_hidden),
+        hidden_grad.reshape(tokens, width_hidden),
+        weight_in,
+        error_in[0],
+        q_prev,
+    )
+    input_grad = ig.reshape(1, -1, patches, width_in)
+    return (input_grad, p_t.T, q_t.astype(f32).T, eo[None])
+
+
 def orthonormal(proj, gram_matrix):
     factor = jnp.linalg.cholesky(gram_matrix)
     return jax.scipy.linalg.solve_triangular(factor, proj.T, lower=True).T
 
 
-def local(inputs, pre_act, hidden_grad, weight_in, error_in, q_prev):
+def staged(inputs, pre_act, hidden_grad, weight_in, error_in, q_prev):
     date_count = lax.axis_size("date")
     width_in = inputs.shape[-1]
     width_hidden = pre_act.shape[-1]
@@ -67,4 +448,23 @@
         P(),
     )
     out_specs = (P("dp", None, "date", None), P("date", None), P(), P("dp", "date", None))
+    n_dp, n_date = mesh.shape["dp"], mesh.shape["date"]
+
+    def local(*args):
+        width_in, width_hidden = args[3].shape
+        rank = args[5].shape[1]
+        direct = (
+            n_date == 4
+            and n_dp * n_date <= 64
+            and args[0].shape[0] == 1
+            and rank % (8 * n_dp) == 0
+            and rank % (16 * n_date) == 0
+            and width_in % (128 * n_date) == 0
+            and width_hidden % (128 * n_dp) == 0
+            and args[0].shape[2] % (8 * n_date) == 0
+        )
+        if direct:
+            return fused(n_dp, n_date, *args)
+        return staged(*args)
+
     return jax.shard_map(local, mesh=mesh, in_specs=in_specs, out_specs=out_specs, check_vma=False)

time: 239 us -> 64.4 us (0.27)
  waiting for transfers between devices: 133 us -> 0 us
  blocking collectives: 54.3 us -> 0 us
  Pallas kernels: 0 us -> 53.2 us
  other arithmetic: 15.8 us -> 0.83 us
  between operations: 14.2 us -> 0.66 us
  matrix products: 10.2 us -> 0 us
  starting transfers between devices: 4.33 us -> 0 us
  local copies, waits for them, and re-layouts: 5.43 us -> 9.05 us
    psum x1 -> x0, waiting for transfers between devices: 114 us -> none  [local(): q_new = lax.psum(right_part, ('dp', 'date')) / lax.axis_size('dp')]
    pallas_call x0 -> x1, Pallas kernels: none -> 53.2 us  [fused(): pl.pallas_call(functools.partial(kernel, n_dp, n_date, patches), out_shap...]
    psum x2 -> x0, blocking collectives: 46.9 us -> none  [the longest x1 29.9 us: local(): proj_rows = lax.psum(jnp.dot(merged_rows, q_prev, precision=highest), 'dp')]
    all_gather x1 -> x0, waiting for transfers between devices: 16.8 us -> none  [local(): lax.all_gather(slope_grad, 'date', axis=0, tiled=True)]
    another operation x5 -> x0, other arithmetic: 12.1 us -> none  [the longest x3 6.52 us: orthonormal(): factor = jnp.linalg.cholesky(gram_matrix)]
    dot_general x6 -> x0, matrix products: 9.98 us -> none  [the longest x1 2.6 us: local(): jnp.dot(p_rows, q_new.T, precision=highest)]
    all_to_all x1 -> x0, blocking collectives: 7.46 us -> none  [local(): lax.all_to_all(local_back.reshape(inputs.shape), 'date', split_axis=2, co...]
    unnamed x14, local copies, waits for them, and re-layouts: 3.86 us -> 9.05 us
  transfers between devices with their start and end apart: 3 -> 0, of which waited for: 3 -> 0; matrix products, arithmetic and copies ran while one was open for 2% -> 0% of each run, Pallas kernels for 0% -> 0%
where the time goes in v1:
time: 64.4 us; the launch traced here: 63.7 us
  Pallas kernels  53.2 us (83%)
  local copies, waits for them, and re-layouts  9.05 us (14%)
  other arithmetic  0.83 us (1%)
  between operations  0.66 us (1%)
    pallas_call x1, Pallas kernels, fused(): pl.pallas_call(functools.partial(kernel, n_dp, n_date, patches), out_shap...  53.2 us
    unnamed x14, local copies, waits for them, and re-layouts  9.05 us

profile of v1, /device:TPU:1, one launch (start us, length us, event | category | flops | bytes accessed | tf_op | source)
XLA Modules:
  0.0 63.7 jit_solution(16850169963360785190)
XLA Ops:
  0.6 1.4 %copy.10.q_hbm = f32[2048,64]{1,0:T(8,128)S(1)} copy(f32[2048,64]{0,1:T(8,128)} %param.11) | data formatting | bytes 1048576 | tf_op args[5]
  2.0 0.0 copy-start
  2.0 1.6 %copy-done = bf16[512,2048]{1,0:T(8,128)(2,1)S(1)} copy-done((bf16[512,2048]{1,0:T(8,128)(2,1)S(1)}, bf16[512,2048]{1,0:T(8,128)(2,1)}, u32[]{:S(2)}) %copy-start) | copy-done | bytes 2097176
  3.6 0.0 copy-start.1
  3.6 1.0 %copy-done.1 = bf16[1,4,32,2048]{3,2,1,0:T(8,128)(2,1)S(1)} copy-done((bf16[1,4,32,2048]{3,2,1,0:T(8,128)(2,1)S(1)}, bf16[1,4,32,2048]{3,2,1,0:T(8,128)(2,1)}, u32[]{:S(2)}) %copy-start.1) | copy-done | bytes 524312
  4.6 0.0 copy-start.2
  4.6 1.0 %copy-done.2 = bf16[1,4,32,2048]{3,2,1,0:T(8,128)(2,1)S(1)} copy-done((bf16[1,4,32,2048]{3,2,1,0:T(8,128)(2,1)S(1)}, bf16[1,4,32,2048]{3,2,1,0:T(8,128)(2,1)}, u32[]{:S(2)}) %copy-start.2) | copy-done | bytes 524312
  5.7 0.0 copy-start.3
  5.7 1.0 %copy-done.3 = bf16[1,128,2048]{2,1,0:T(8,128)(2,1)S(1)} copy-done((bf16[1,128,2048]{2,1,0:T(8,128)(2,1)S(1)}, bf16[1,128,2048]{2,1,0:T(8,128)(2,1)}, u32[]{:S(2)}) %copy-start.3) | copy-done | bytes 524312
  6.7 0.0 copy-start.4
  6.7 0.9 %copy-done.4 = bf16[1,4,32,512]{3,2,1,0:T(8,128)(2,1)S(1)} copy-done((bf16[1,4,32,512]{3,2,1,0:T(8,128)(2,1)S(1)}, bf16[1,4,32,512]{3,2,1,0:T(8,128)(2,1)}, u32[]{:S(2)}) %copy-start.4) | copy-done | bytes 131096
  7.6 53.2 %shard_map.93 = (bf16[128,512]{1,0:T(8,128)(2,1)S(1)}, f32[64,128]{1,0:T(8,128)S(1)}, bf16[64,2048]{1,0:T(8,128)(2,1)S(1)}, bf16[128,2048]{1,0:T(8,128)(2,1)S(1)}) custom-call(bf16[128,512]{1,0:T(8,128)(2,1)S(1)} %bitcast.13, bf16[128,2048]{1,0:T(8,128)(2,1)S(1)} %bitcast.9, bf16[128,2048]{1,0:T(8,128)(2,1)S(1)} %bitcast.10, bf16[512,2048]{1,0:T(8,128)(2,1)S(1)} %copy-done, ...), custom_call_target="tpu_custom_call" | custom-call | tf_op jit(solution)/shard_map/pallas_call | solution.py:347
  60.9 0.8 %convert_bitcast_fusion = f32[2048,64]{0,1:T(8,128)} fusion(bf16[64,2048]{1,0:T(8,128)(2,1)S(1)} %get-tuple-element.10), kind=kLoop, calls=%fused_computation | loop fusion | flops 131072 | bytes 786432 | tf_op jit(solution)/shard_map/transpose | solution.py:397
  61.7 0.7 %copy.14 = bf16[1,16,8,512]{3,2,1,0:T(8,128)(2,1)} copy(bf16[1,16,8,512]{3,2,1,0:T(8,128)(2,1)S(1)} %bitcast.14) | data formatting | bytes 262144
  62.3 0.6 copy.15
  63.0 0.8 %copy.16 = bf16[1,128,2048]{2,1,0:T(8,128)(2,1)} copy(bf16[1,128,2048]{2,1,0:T(8,128)(2,1)S(1)} %bitcast.12) | data formatting | bytes 1048576
Async XLA Ops:
  2.0 1.6 %copy-start = (bf16[512,2048]{1,0:T(8,128)(2,1)S(1)}, bf16[512,2048]{1,0:T(8,128)(2,1)}, u32[]{:S(2)}) copy-start(bf16[512,2048]{1,0:T(8,128)(2,1)} %w_hbm.1) | copy-start | bytes 6291460
  3.6 1.0 %copy-start.1 = (bf16[1,4,32,2048]{3,2,1,0:T(8,128)(2,1)S(1)}, bf16[1,4,32,2048]{3,2,1,0:T(8,128)(2,1)}, u32[]{:S(2)}) copy-start(bf16[1,4,32,2048]{3,2,1,0:T(8,128)(2,1)} %param.7) | copy-start | bytes 1572868
  4.6 1.0 %copy-start.2 = (bf16[1,4,32,2048]{3,2,1,0:T(8,128)(2,1)S(1)}, bf16[1,4,32,2048]{3,2,1,0:T(8,128)(2,1)}, u32[]{:S(2)}) copy-start(bf16[1,4,32,2048]{3,2,1,0:T(8,128)(2,1)} %param.8) | copy-start | bytes 1572868
  5.7 1.0 %copy-start.3 = (bf16[1,128,2048]{2,1,0:T(8,128)(2,1)S(1)}, bf16[1,128,2048]{2,1,0:T(8,128)(2,1)}, u32[]{:S(2)}) copy-start(bf16[1,128,2048]{2,1,0:T(8,128)(2,1)} %param.10) | copy-start | bytes 1572868
  6.7 0.9 %copy-start.4 = (bf16[1,4,32,512]{3,2,1,0:T(8,128)(2,1)S(1)}, bf16[1,4,32,512]{3,2,1,0:T(8,128)(2,1)}, u32[]{:S(2)}) copy-start(bf16[1,4,32,512]{3,2,1,0:T(8,128)(2,1)} %param.6) | copy-start | bytes 393220

commit v2 on v1

--- a/solution.py
+++ b/solution.py
@@ -7,6 +7,7 @@
 from jax.experimental.pallas import tpu as pltpu
 from jax.sharding import PartitionSpec as P
 
+panel = 8
 inv_root2 = 0.7071067811865476
 inv_root_twopi = 0.3989422804014327
 highest = lax.Precision.HIGHEST
@@ -43,15 +44,24 @@
     table = jnp.concatenate([gram, eye], axis=1)
     blocks = [table[8 * i : 8 * i + 8] for i in range(rank // 8)]
     sub = lax.broadcasted_iota(jnp.int32, (8, 2 * rank), 0)
-    for k in range(rank):
-        i, r = divmod(k, 8)
-        row = blocks[i][r : r + 1, :]
-        row = row * (1.0 / row[:, k : k + 1])
-        for j in range(i, rank // 8):
-            update = blocks[j][:, k : k + 1] * row
-            if j == i:
-                update = jnp.where(sub > r, update, 0.0)
-            blocks[j] = blocks[j] - update
+    for k in range(0, rank, panel):
+        i = k // 8
+        cols = {
+            j: [jnp.broadcast_to(blocks[j][:, k + m : k + m + 1], sub.shape) for m in range(panel)]
+            for j in range(i, rank // 8)
+        }
+        for m in range(panel):
+            r = (k + m) % 8
+            row = blocks[i][r : r + 1, :]
+            inverse = 1.0 / cols[i][m][r : r + 1, :]
+            heads = [cols[i][n][r : r + 1, :] for n in range(panel)]
+            for j in range(i, rank // 8):
+                factor = cols[j][m] * inverse
+                if j == i:
+                    factor = jnp.where(sub > r, factor, 0.0)
+                for n in range(m + 1, panel):
+                    cols[j][n] = cols[j][n] - factor * heads[n]
+                blocks[j] = blocks[j] - factor * row
     table = jnp.concatenate(blocks, axis=0)
     pivots = jnp.sum(table[:, :rank] * eye, axis=1, keepdims=True)
     return dot(table[:, rank:] * lax.rsqrt(pivots), proj_t, 1, 0, highest)
@@ -67,10 +77,10 @@
     w_hbm,
     err_hbm,
     q_hbm,
-    ig_ref,
-    p_ref,
-    qn_ref,
-    eo_ref,
+    ig_out,
+    p_out,
+    qn_out,
+    merged_out,
     x_v,
     pre_v,
     hid_v,
@@ -89,7 +99,9 @@
     right_recv,
     right_full,
     merged,
+    ig_ref,
     load_sem,
+    store_sem,
     slope_send,
     slope_recv,
     xcol_send,
@@ -107,7 +119,7 @@
 ):
     tokens, width_in = x_v.shape
     width_hidden = stack.shape[1]
-    rank = q_v.shape[1]
+    rank = q_v.shape[0]
     cols_own = width_in // n_date
     scale = (tokens * n_date) ** (-0.5)
     pa = rank // n_dp
@@ -171,7 +183,7 @@
             stack[rows, :] = (hid_v[rows, :].astype(f32) * gelu_slope(pre_v[rows, :])).astype(bf16)
         if c == 0:
             pl.semaphore_wait(barrier, len(others))
-        for kind in (1, 0):
+        for kind in (1, 0) if c == 0 else (0,):
             copy = slope_copy(c, kind)
             copy.start()
             sent.append(copy)
@@ -180,13 +192,13 @@
     loads[5].wait()
     q_high, q_low = parts(q_v[...])
     both = stack[...]
-    seen = dot(both, q_high, 1, 0) + dot(both, q_low, 1, 0)
+    seen = dot(q_high, both, 1, 1) + dot(q_low, both, 1, 1)
     loads[6].wait()
     x = x_v[...]
-    y_high, y_low = parts(seen[:tokens] * scale)
-    proj_part[...] = dot(y_high, x, 0, 0) + dot(y_low, x, 0, 0)
+    y_high, y_low = parts(seen[:, :tokens] * scale)
+    proj_part[...] = dot(y_high, x, 1, 0) + dot(y_low, x, 1, 0)
     own_cols = pl.ds(pl.multiple_of(date * cols_own, cols_own), cols_own)
-    proj_part[:, own_cols] += seen[tokens:].T
+    proj_part[:, own_cols] += seen[:, tokens:]
 
     def proj_tile(ref, i, j):
         return ref.at[
@@ -253,10 +265,14 @@
         source = (lax.rem(dp - o[0] + n_dp, n_dp), lax.rem(date - o[1] + n_date, n_date))
         tile = proj_tile(proj_full, *source)
         remote(tile, tile, pg_send.at[n], pg_recv.at[n], target(o)).wait_recv()
+    copy = slope_copy(1, 1)
+    copy.start()
+    sent.append(copy)
     p_all = whiten(proj_full[...])
     p_full[...] = p_all
     p_own = p_full[:, own_cols]
-    p_ref[...] = p_own
+    stores = [pltpu.make_async_copy(p_full.at[:, own_cols], p_out, store_sem.at[0])]
+    stores[0].start()
     p_high, p_low = parts(p_all)
     z = (dot(p_high, x, 1, 1) + dot(p_low, x, 1, 1)) * scale
     left_high, left_low = parts(jnp.concatenate([z, p_own], axis=1))
@@ -316,19 +332,56 @@
     for c in range(2):
         slope_copy(c, 2).wait_recv()
     merged[...] += add_peer(2, diag)
-    own_high, own_low = parts(p_own)
+    stores.append(pltpu.make_async_copy(ig_ref, ig_out, store_sem.at[1]))
+    stores.append(pltpu.make_async_copy(merged, merged_out, store_sem.at[2]))
+    stores[1].start()
+    stores[2].start()
 
     for o in others:
         n = slot(o)
         source = (lax.rem(dp - o[0] + n_dp, n_dp), lax.rem(date - o[1] + n_date, n_date))
         tile = right_tile(right_full, *source)
         remote(tile, tile, qg_send.at[n], qg_recv.at[n], target(o)).wait_recv()
-    q_new = right_full[...]
-    qn_ref[...] = q_new
-    low_rank = dot(own_high, q_new, 0, 0) + dot(own_low, q_new, 0, 0)
-    eo_ref[...] = (merged[...] - low_rank).astype(bf16)
+    stores.append(pltpu.make_async_copy(right_full, qn_out, store_sem.at[3]))
+    stores[3].start()
+    for copy in stores:
+        copy.wait()
     for copy in sent:
         copy.wait_send()
+
+
+def finish(
+    ig_hbm, p_hbm, q_hbm, merged_hbm, ig_out, p_out, q_out, eo_out, ig_v, p_v, q_v, wide_v,
+    merged_v, eo_v, load_sem, store_sem
+):
+    rows = merged_v.shape[0] // 4
+    cuts = [pl.ds(c * rows, rows) for c in range(4)]
+    pairs = [(p_hbm, p_v), (q_hbm, q_v)]
+    pairs += [(merged_hbm.at[cut], merged_v.at[cut]) for cut in cuts]
+    pairs += [(ig_hbm, ig_v)]
+    loads = [pltpu.make_async_copy(s, d, load_sem.at[n]) for n, (s, d) in enumerate(pairs)]
+    for copy in loads:
+        copy.start()
+    pairs = [(p_v, p_out), (wide_v, q_out)]
+    pairs += [(eo_v.at[cut], eo_out.at[cut]) for cut in cuts]
+    pairs += [(ig_v, ig_out)]
+    stores = [pltpu.make_async_copy(s, d, store_sem.at[n]) for n, (s, d) in enumerate(pairs)]
+    loads[0].wait()
+    stores[0].start()
+    loads[1].wait()
+    wide_v[...] = q_v[...].astype(f32)
+    stores[1].start()
+    p_high, p_low = parts(p_v[...])
+    for c, cut in enumerate(cuts):
+        loads[2 + c].wait()
+        p_rows = slice(c * rows, (c + 1) * rows)
+        low_rank = dot(p_high[:, p_rows], q_v[...], 0, 0) + dot(p_low[:, p_rows], q_v[...], 0, 0)
+        eo_v[cut, :] = (merged_v[cut, :] - low_rank).astype(bf16)
+        stores[2 + c].start()
+    loads[6].wait()
+    stores[6].start()
+    for copy in stores:
+        copy.wait()
 
 
 def fused(n_dp, n_date, inputs, pre_act, hidden_grad, weight_in, error_in, q_prev):
@@ -340,27 +393,26 @@
     cols_own = width_in // n_date
     patches = inputs.shape[2] // n_date
     ig_rows = inputs.shape[1] * patches
-    any_spec = pl.BlockSpec(memory_space=pl.ANY)
-    vmem_spec = pl.BlockSpec(memory_space=pltpu.VMEM)
+    hbm_spec = pl.BlockSpec(memory_space=pltpu.HBM)
     dma = pltpu.SemaphoreType.DMA
     qa, qb = width_hidden // n_dp, rank // n_date
-    ig, p_t, q_t, eo = pl.pallas_call(
+    ig, p_t, q_t, merged = pl.pallas_call(
         functools.partial(kernel, n_dp, n_date, patches),
         out_shape=(
             jax.ShapeDtypeStruct((n_date * ig_rows, width_in), bf16),
             jax.ShapeDtypeStruct((rank, cols_own), f32),
             jax.ShapeDtypeStruct((rank, width_hidden), bf16),
-            jax.ShapeDtypeStruct((cols_own, width_hidden), bf16),
+            jax.ShapeDtypeStruct((cols_own, width_hidden), f32),
         ),
-        in_specs=[any_spec] * 6,
-        out_specs=(vmem_spec,) * 4,
+        in_specs=[hbm_spec] * 6,
+        out_specs=(hbm_spec,) * 4,
         scratch_shapes=[
             pltpu.VMEM((tokens, width_in), bf16),
             pltpu.VMEM((tokens, width_hidden), bf16),
             pltpu.VMEM((tokens, width_hidden), bf16),
             pltpu.VMEM((width_in, width_hidden), bf16),
             pltpu.VMEM((tokens + cols_own, width_hidden), bf16),
-            pltpu.VMEM((width_hidden, rank), f32),
+            pltpu.VMEM((rank, width_hidden), f32),
             pltpu.VMEM((3, tokens, width_hidden), bf16),
             pltpu.VMEM((n_date, tokens, cols_own), bf16),
             pltpu.VMEM((n_date, ig_rows, width_in), bf16),
@@ -373,7 +425,9 @@
             pltpu.VMEM((n, qb, qa), bf16),
             pltpu.VMEM((rank, width_hidden), bf16),
             pltpu.VMEM((cols_own, width_hidden), f32),
+            pltpu.VMEM((n_date * ig_rows, width_in), bf16),
             dma((8,)),
+            dma((4,)),
             dma((6,)),
             dma((6,)),
             dma((n_date,)),
@@ -383,7 +437,7 @@
         ]
         + [dma((n,))] * 8,
         compiler_params=pltpu.CompilerParams(
-            collective_id=0, has_side_effects=True, vmem_limit_bytes=48 * 1024 * 1024
+            collective_id=0, has_side_effects=True, vmem_limit_bytes=64 * 1024 * 1024
         ),
     )(
         x,
@@ -391,10 +445,32 @@
         hidden_grad.reshape(tokens, width_hidden),
         weight_in,
         error_in[0],
-        q_prev,
+        q_prev.T,
     )
+    ig, p_t, q_t, error_out = pl.pallas_call(
+        finish,
+        out_shape=(
+            jax.ShapeDtypeStruct(ig.shape, bf16),
+            jax.ShapeDtypeStruct(p_t.shape, f32),
+            jax.ShapeDtypeStruct(q_t.shape, f32),
+            jax.ShapeDtypeStruct(merged.shape, bf16),
+        ),
+        in_specs=[hbm_spec] * 4,
+        out_specs=(hbm_spec,) * 4,
+        scratch_shapes=[
+            pltpu.VMEM(ig.shape, bf16),
+            pltpu.VMEM(p_t.shape, f32),
+            pltpu.VMEM(q_t.shape, bf16),
+            pltpu.VMEM(q_t.shape, f32),
+            pltpu.VMEM(merged.shape, f32),
+            pltpu.VMEM(merged.shape, bf16),
+            dma((7,)),
+            dma((7,)),
+        ],
+        compiler_params=pltpu.CompilerParams(vmem_limit_bytes=64 * 1024 * 1024),
+    )(ig, p_t, q_t, merged)
     input_grad = ig.reshape(1, -1, patches, width_in)
-    return (input_grad, p_t.T, q_t.astype(f32).T, eo[None])
+    return (input_grad, p_t.T, q_t.T, error_out[None])
 
 
 def orthonormal(proj, gram_matrix):

time: 64.4 us -> 48.1 us (0.75)
  local copies, waits for them, and re-layouts: 9.05 us -> 0 us
  Pallas kernels: 53.2 us -> 47 us
  other arithmetic: 0.83 us -> 0 us
    pallas_call x1, Pallas kernels: 53.2 us -> 43.9 us  [fused(): pl.pallas_call(functools.partial(kernel, n_dp, n_date, patches), out_shap...]
    unnamed x14 -> x0, local copies, waits for them, and re-layouts: 9.05 us -> none
    pallas_call x0 -> x1, Pallas kernels: none -> 3.11 us  [fused(): pl.pallas_call(finish, out_shape=(jax.ShapeDtypeStruct(ig.shape, bf16), j...]
    transpose x1 -> x0, other arithmetic: 0.83 us -> none  [fused(): return (input_grad, p_t.T, q_t.astype(f32).T, eo[None])]
where the time goes in v2:
time: 48.1 us; the launch traced here: 47.6 us
  Pallas kernels  47 us (98%)
  between operations  0.64 us (1%)
    pallas_call x1, Pallas kernels, fused(): pl.pallas_call(functools.partial(kernel, n_dp, n_date, patches), out_shap...  43.9 us
    pallas_call x1, Pallas kernels, fused(): pl.pallas_call(finish, out_shape=(jax.ShapeDtypeStruct(ig.shape, bf16), j...  3.11 us

profile of v2, /device:TPU:1, one launch (start us, length us, event | category | flops | bytes accessed | tf_op | source)
XLA Modules:
  0.0 47.6 jit_solution(10793915292590062606)
XLA Ops:
  0.6 43.9 %shard_map.93 = (bf16[128,512]{1,0:T(8,128)(2,1)}, f32[64,128]{1,0:T(8,128)}, bf16[64,2048]{1,0:T(8,128)(2,1)}, f32[128,2048]{1,0:T(8,128)}) custom-call(bf16[128,512]{1,0:T(8,128)(2,1)} %bitcast.13, bf16[128,2048]{1,0:T(8,128)(2,1)} %bitcast.9, bf16[128,2048]{1,0:T(8,128)(2,1)} %bitcast.10, bf16[512,2048]{1,0:T(8,128)(2,1)} %w_hbm.1, ...), custom_call_target="tpu_custom_call" | custom-call | tf_op jit(solution)/shard_map/pallas_call | solution.py:399
  44.5 3.1 %shard_map.94 = (bf16[128,512]{1,0:T(8,128)(2,1)}, f32[64,128]{1,0:T(8,128)}, f32[64,2048]{1,0:T(8,128)}, bf16[128,2048]{1,0:T(8,128)(2,1)}) custom-call(bf16[128,512]{1,0:T(8,128)(2,1)} %get-tuple-element.12.ig_hbm, f32[64,128]{1,0:T(8,128)} %get-tuple-element.13.p_hbm, bf16[64,2048]{1,0:T(8,128)(2,1)} %get-tuple-element.14.q_hbm, ...), custom_call_target="tpu_custom_call" | custom-call | tf_op jit(solution)/shard_map/pallas_call | solution.py:450

commit v3 on v2

--- a/solution.py
+++ b/solution.py
@@ -100,8 +100,16 @@
     right_full,
     merged,
     ig_ref,
+    proj_swap,
+    proj_half,
+    right_all,
+    right_swap,
+    right_sum,
+    right_half,
     load_sem,
     store_sem,
+    swap_send,
+    swap_recv,
     slope_send,
     slope_recv,
     xcol_send,
@@ -129,6 +137,14 @@
     date = lax.axis_index("date")
     others = [(i, j) for i in range(n_dp) for j in range(n_date) if i + j > 0]
     others = sorted(others, key=lambda o: -min(o[0], n_dp - o[0]))
+    same_core = [o for o in others if o[1] % 2 == 0]
+    proj_to = others
+    right_to = same_core
+    core = lax.rem(date, 2)
+    chips = n_date // 2
+
+    def place(j):
+        return lax.rem(j, 2) * chips + lax.div(j, 2)
 
     def slot(o):
         return o[0] * n_date + o[1]
@@ -196,23 +212,36 @@
     loads[6].wait()
     x = x_v[...]
     y_high, y_low = parts(seen[:, :tokens] * scale)
-    proj_part[...] = dot(y_high, x, 1, 0) + dot(y_low, x, 1, 0)
+    part = dot(y_high, x, 1, 0) + dot(y_low, x, 1, 0)
+    for j in range(n_date):
+        proj_part[j % 2 * chips + j // 2] = part[:, j * cols_own : (j + 1) * cols_own]
+    proj_part[place(date)] += seen[:, tokens:]
+
     own_cols = pl.ds(pl.multiple_of(date * cols_own, cols_own), cols_own)
-    proj_part[:, own_cols] += seen[:, tokens:]
-
-    def proj_tile(ref, i, j):
-        return ref.at[
-            pl.ds(pl.multiple_of(i * pa, pa), pa),
-            pl.ds(pl.multiple_of(j * cols_own, cols_own), cols_own),
-        ]
+    my_blocks = pl.ds(core * chips, chips)
+    mate_blocks = pl.ds((1 - core) * chips, chips)
+    swap = remote(
+        proj_part.at[mate_blocks], proj_swap, swap_send.at[0], swap_recv.at[0], (dp, mate)
+    )
+    swap.start()
+    sent.append(swap)
+    swap.wait_recv()
+    proj_half[...] = proj_part[my_blocks] + proj_swap[...]
+
+    def proj_rows(i):
+        return pl.ds(pl.multiple_of(i * pa, pa), pa)
+
+    def half_tile(i, j):
+        return proj_half.at[lax.div(j, 2), proj_rows(i)]
+
+    def proj_tile(i, j):
+        return proj_full.at[place(j), proj_rows(i)]
 
     reduce_copies = []
-    for o in others:
+    for o in same_core:
         n = slot(o)
         to = target(o)
-        copy = remote(
-            proj_tile(proj_part, *to), proj_recv.at[n], pr_send.at[n], pr_recv.at[n], to
-        )
+        copy = remote(half_tile(*to), proj_recv.at[n], pr_send.at[n], pr_recv.at[n], to)
         copy.start()
         reduce_copies.append(copy)
         sent.append(copy)
@@ -245,13 +274,13 @@
         ig_copies.append(copy)
         sent.append(copy)
 
-    total = proj_tile(proj_part, dp, date)[...]
-    for o, copy in zip(others, reduce_copies):
+    total = half_tile(dp, date)[...]
+    for o, copy in zip(same_core, reduce_copies):
         copy.wait_recv()
         total = total + proj_recv[slot(o)]
-    mine = proj_tile(proj_full, dp, date)
+    mine = proj_tile(dp, date)
     mine[...] = total
-    for o in others:
+    for o in proj_to:
         n = slot(o)
         copy = remote(mine, mine, pg_send.at[n], pg_recv.at[n], target(o))
         copy.start()
@@ -260,15 +289,25 @@
     xcol = x_v[:, own_cols]
     merged[...] = stack[tokens:, :].astype(f32) + dot(xcol, stack[:tokens, :], 0, 0) * scale
 
-    for o in others:
+    for o in proj_to:
         n = slot(o)
         source = (lax.rem(dp - o[0] + n_dp, n_dp), lax.rem(date - o[1] + n_date, n_date))
-        tile = proj_tile(proj_full, *source)
+        tile = proj_tile(*source)
         remote(tile, tile, pg_send.at[n], pg_recv.at[n], target(o)).wait_recv()
+    if proj_to is same_core:
+        blocks = proj_full.at[my_blocks]
+        copy = remote(blocks, blocks, swap_send.at[1], swap_recv.at[1], (dp, mate))
+        copy.start()
+        sent.append(copy)
+        blocks = proj_full.at[mate_blocks]
+        remote(blocks, blocks, swap_send.at[1], swap_recv.at[1], (dp, mate)).wait_recv()
     copy = slope_copy(1, 1)
     copy.start()
     sent.append(copy)
-    p_all = whiten(proj_full[...])
+    proj_t = jnp.concatenate(
+        [proj_full[j % 2 * chips + j // 2] for j in range(n_date)], axis=1
+    )
+    p_all = whiten(proj_t)
     p_full[...] = p_all
     p_own = p_full[:, own_cols]
     stores = [pltpu.make_async_copy(p_full.at[:, own_cols], p_out, store_sem.at[0])]
@@ -277,7 +316,18 @@
     z = (dot(p_high, x, 1, 1) + dot(p_low, x, 1, 1)) * scale
     left_high, left_low = parts(jnp.concatenate([z, p_own], axis=1))
     right = dot(left_high, both, 1, 0) + dot(left_low, both, 1, 0)
+    right_all[...] = right
     right_send[...] = right.astype(bf16)
+    my_rows = pl.ds(pl.multiple_of(core * (rank // 2), rank // 2), rank // 2)
+    mate_rows = pl.ds(pl.multiple_of((1 - core) * (rank // 2), rank // 2), rank // 2)
+    swap = remote(
+        right_send.at[mate_rows], right_swap, swap_send.at[2], swap_recv.at[2], (dp, mate)
+    )
+    swap.start()
+    sent.append(swap)
+    swap.wait_recv()
+    right_sum[...] = right_all[my_rows, :] + right_swap[...].astype(f32)
+    right_half[...] = right_sum[...].astype(bf16)
 
     def right_tile(ref, i, j):
         return ref.at[
@@ -285,11 +335,12 @@
         ]
 
     reduce_copies = []
-    for o in others:
+    for o in same_core:
         n = slot(o)
         to = target(o)
+        tile = right_tile(right_half, to[0], lax.div(to[1], 2))
         copy = remote(
-            right_tile(right_send, *to), right_recv.at[n], qr_send.at[n], qr_recv.at[n], to
+            tile, right_recv.at[n], qr_send.at[n], qr_recv.at[n], to
         )
         copy.start()
         reduce_copies.append(copy)
@@ -311,13 +362,13 @@
         slope_copy(c, 0).wait_recv()
     merged[...] += add_peer(0, mate) + add_peer(1, across)
 
-    total = right_tile(right_send, dp, date)[...].astype(f32)
-    for o, copy in zip(others, reduce_copies):
+    total = right_tile(right_sum, dp, lax.div(date, 2))[...]
+    for o, copy in zip(same_core, reduce_copies):
         copy.wait_recv()
         total = total + right_recv[slot(o)].astype(f32)
-    mine = right_tile(right_full, dp, date)
+    mine = right_tile(right_full, dp, place(date))
     mine[...] = (total * (1.0 / n_dp)).astype(bf16)
-    for o in others:
+    for o in right_to:
         n = slot(o)
         copy = remote(mine, mine, qg_send.at[n], qg_recv.at[n], target(o))
         copy.start()
@@ -337,11 +388,18 @@
     stores[1].start()
     stores[2].start()
 
-    for o in others:
+    for o in right_to:
         n = slot(o)
         source = (lax.rem(dp - o[0] + n_dp, n_dp), lax.rem(date - o[1] + n_date, n_date))
-        tile = right_tile(right_full, *source)
+        tile = right_tile(right_full, source[0], place(source[1]))
         remote(tile, tile, qg_send.at[n], qg_recv.at[n], target(o)).wait_recv()
+    if right_to is same_core:
+        rows = right_full.at[my_rows]
+        copy = remote(rows, rows, swap_send.at[3], swap_recv.at[3], (dp, mate))
+        copy.start()
+        sent.append(copy)
+        rows = right_full.at[mate_rows]
+        remote(rows, rows, swap_send.at[3], swap_recv.at[3], (dp, mate)).wait_recv()
     stores.append(pltpu.make_async_copy(right_full, qn_out, store_sem.at[3]))
     stores[3].start()
     for copy in stores:
@@ -417,16 +475,24 @@
             pltpu.VMEM((n_date, tokens, cols_own), bf16),
             pltpu.VMEM((n_date, ig_rows, width_in), bf16),
             pltpu.VMEM((n_date, ig_rows, width_in), bf16),
-            pltpu.VMEM((rank, width_in), f32),
+            pltpu.VMEM((n_date, rank, cols_own), f32),
             pltpu.VMEM((n, rank // n_dp, cols_own), f32),
-            pltpu.VMEM((rank, width_in), f32),
+            pltpu.VMEM((n_date, rank, cols_own), f32),
             pltpu.VMEM((rank, width_in), f32),
             pltpu.VMEM((rank, width_hidden), bf16),
             pltpu.VMEM((n, qb, qa), bf16),
             pltpu.VMEM((rank, width_hidden), bf16),
             pltpu.VMEM((cols_own, width_hidden), f32),
             pltpu.VMEM((n_date * ig_rows, width_in), bf16),
+            pltpu.VMEM((n_date // 2, rank, cols_own), f32),
+            pltpu.VMEM((n_date // 2, rank, cols_own), f32),
+            pltpu.VMEM((rank, width_hidden), f32),
+            pltpu.VMEM((rank // 2, width_hidden), bf16),
+            pltpu.VMEM((rank // 2, width_hidden), f32),
+            pltpu.VMEM((rank // 2, width_hidden), bf16),
             dma((8,)),
+            dma((4,)),
+            dma((4,)),
             dma((4,)),
             dma((6,)),
             dma((6,)),

time: 48.1 us -> 44.5 us (0.925)
  Pallas kernels: 47 us -> 43.7 us
    pallas_call x1, Pallas kernels: 43.9 us -> 40.6 us  [fused(): pl.pallas_call(functools.partial(kernel, n_dp, n_date, patches), out_shap...]
where the time goes in v3:
time: 44.5 us; the launch traced here: 44.3 us
  Pallas kernels  43.7 us (98%)
  between operations  0.64 us (1%)
    pallas_call x1, Pallas kernels, fused(): pl.pallas_call(functools.partial(kernel, n_dp, n_date, patches), out_shap...  40.6 us
    pallas_call x1, Pallas kernels, fused(): pl.pallas_call(finish, out_shape=(jax.ShapeDtypeStruct(ig.shape, bf16), j...  3.11 us

profile of v3, /device:TPU:1, one launch (start us, length us, event | category | flops | bytes accessed | tf_op | source)
XLA Modules:
  0.0 44.3 jit_solution(2572420292656378053)
XLA Ops:
  0.6 40.6 %shard_map.93 = (bf16[128,512]{1,0:T(8,128)(2,1)}, f32[64,128]{1,0:T(8,128)}, bf16[64,2048]{1,0:T(8,128)(2,1)}, f32[128,2048]{1,0:T(8,128)}) custom-call(bf16[128,512]{1,0:T(8,128)(2,1)} %bitcast.13, bf16[128,2048]{1,0:T(8,128)(2,1)} %bitcast.9, bf16[128,2048]{1,0:T(8,128)(2,1)} %bitcast.10, bf16[512,2048]{1,0:T(8,128)(2,1)} %w_hbm.1, ...), custom_call_target="tpu_custom_call" | custom-call | tf_op jit(solution)/shard_map/pallas_call | solution.py:457
  41.2 3.1 %shard_map.94 = (bf16[128,512]{1,0:T(8,128)(2,1)}, f32[64,128]{1,0:T(8,128)}, f32[64,2048]{1,0:T(8,128)}, bf16[128,2048]{1,0:T(8,128)(2,1)}) custom-call(bf16[128,512]{1,0:T(8,128)(2,1)} %get-tuple-element.12.ig_hbm, f32[64,128]{1,0:T(8,128)} %get-tuple-element.13.p_hbm, bf16[64,2048]{1,0:T(8,128)(2,1)} %get-tuple-element.14.q_hbm, ...), custom_call_target="tpu_custom_call" | custom-call | tf_op jit(solution)/shard_map/pallas_call | solution.py:516

commit v4 on v3

--- a/solution.py
+++ b/solution.py
@@ -346,22 +346,6 @@
         reduce_copies.append(copy)
         sent.append(copy)
 
-    for c in range(2):
-        slope_copy(c, 1).wait_recv()
-        copy = slope_copy(c, 2)
-        copy.start()
-        sent.append(copy)
-    for copy in x_copies:
-        copy.wait_recv()
-
-    def add_peer(kind, peer):
-        off = lax.rem(date - peer + n_date, n_date)
-        return dot(xcols[off], slopes[kind], 0, 0) * scale
-
-    for c in range(2):
-        slope_copy(c, 0).wait_recv()
-    merged[...] += add_peer(0, mate) + add_peer(1, across)
-
     total = right_tile(right_sum, dp, lax.div(date, 2))[...]
     for o, copy in zip(same_core, reduce_copies):
         copy.wait_recv()
@@ -373,6 +357,22 @@
         copy = remote(mine, mine, qg_send.at[n], qg_recv.at[n], target(o))
         copy.start()
         sent.append(copy)
+
+    for c in range(2):
+        slope_copy(c, 1).wait_recv()
+        copy = slope_copy(c, 2)
+        copy.start()
+        sent.append(copy)
+    for copy in x_copies:
+        copy.wait_recv()
+
+    def add_peer(kind, peer):
+        off = lax.rem(date - peer + n_date, n_date)
+        return dot(xcols[off], slopes[kind], 0, 0) * scale
+
+    for c in range(2):
+        slope_copy(c, 0).wait_recv()
+    merged[...] += add_peer(0, mate) + add_peer(1, across)
 
     ig_rows = back_send.shape[1]
     for off, copy in zip(range(1, n_date), ig_copies):

time: 44.5 us -> 44.5 us (level)
  no operation moved by 1% of the time
where the time goes in v4:
time: 44.5 us; the launch traced here: 44.3 us
  Pallas kernels  43.7 us (98%)
  between operations  0.64 us (1%)
    pallas_call x1, Pallas kernels, fused(): pl.pallas_call(functools.partial(kernel, n_dp, n_date, patches), out_shap...  40.6 us
    pallas_call x1, Pallas kernels, fused(): pl.pallas_call(finish, out_shape=(jax.ShapeDtypeStruct(ig.shape, bf16), j...  3.11 us

profile of v4, /device:TPU:1, one launch (start us, length us, event | category | flops | bytes accessed | tf_op | source)
XLA Modules:
  0.0 44.3 jit_solution(13543699285384161480)
XLA Ops:
  0.6 40.6 %shard_map.93 = (bf16[128,512]{1,0:T(8,128)(2,1)}, f32[64,128]{1,0:T(8,128)}, bf16[64,2048]{1,0:T(8,128)(2,1)}, f32[128,2048]{1,0:T(8,128)}) custom-call(bf16[128,512]{1,0:T(8,128)(2,1)} %bitcast.13, bf16[128,2048]{1,0:T(8,128)(2,1)} %bitcast.9, bf16[128,2048]{1,0:T(8,128)(2,1)} %bitcast.10, bf16[512,2048]{1,0:T(8,128)(2,1)} %w_hbm.1, ...), custom_call_target="tpu_custom_call" | custom-call | tf_op jit(solution)/shard_map/pallas_call | solution.py:457
  41.2 3.1 %shard_map.94 = (bf16[128,512]{1,0:T(8,128)(2,1)}, f32[64,128]{1,0:T(8,128)}, f32[64,2048]{1,0:T(8,128)}, bf16[128,2048]{1,0:T(8,128)(2,1)}) custom-call(bf16[128,512]{1,0:T(8,128)(2,1)} %get-tuple-element.12.ig_hbm, f32[64,128]{1,0:T(8,128)} %get-tuple-element.13.p_hbm, bf16[64,2048]{1,0:T(8,128)(2,1)} %get-tuple-element.14.q_hbm, ...), custom_call_target="tpu_custom_call" | custom-call | tf_op jit(solution)/shard_map/pallas_call | solution.py:516
